TPU v7x, 32 devices: a whole 2x2x4 slice. The times are simulated.
32 devices in a mesh: grp: 4 (over y, core), shard: 4 (over z), side: 2 (over x).
Axes of the slice: x: 2, y: 2, z: 4, core: 2. Of those that a mesh axis runs over, the one named last changes fastest.
Arguments:
- tokens: bfloat16 [512, 4096], P(('grp', 'side')), may hold values from -6 to 6
- routes: int32 [512, 2], P(('grp', 'side')), may hold values from 0 to 3, all different within a row; in each aligned block of 64 rows (0 to 63, 64 to 127, ...) at most 64 rows name the same one
- probs: float32 [512, 2], P(('grp', 'side')), may hold values from 0.02 to 1
- w_gate: bfloat16 [16, 4096, 256], P(('grp', 'shard')), may hold values from -0.09375 to 0.09375
- w_up: bfloat16 [16, 4096, 256], P(('grp', 'shard')), may hold values from -0.09375 to 0.09375
- w_down: bfloat16 [16, 256, 4096], P(('grp', 'shard')), may hold values from -0.1875 to 0.1875
Outputs:
- mixed: bfloat16 [512, 4096], P(('grp', 'side'), 'shard')
Inputs may be any that keep to these rules, and one draw needn't show every extreme that they name: `routes`: each token names 2 different experts. Within each aligned block of 64 tokens no expert is named by more than 64 tokens, a bound that some block reaches.
All inputs are finite; a program needn't handle non-finite values.
Results may differ from a plain program's by a relative error of at most 0.0057.
Values may be sent and summed in bfloat16 or wider, within the bound.
A program may use at most 64 MiB of HBM per device.

v0:
```python
import jax
import jax.numpy as jnp
from jax import lax
from jax.sharding import PartitionSpec as P

TPE = 4


def tile_pass(rows, w_gate, w_up, w_down):
    flat = rows.reshape(-1, rows.shape[2])
    gate = jnp.dot(flat, w_gate[0], preferred_element_type=jnp.float32)
    upper = jnp.dot(flat, w_up[0], preferred_element_type=jnp.float32)
    hidden = (jax.nn.silu(gate) * upper).astype(jnp.bfloat16)
    result = jnp.dot(hidden, w_down[0], preferred_element_type=jnp.float32).astype(jnp.bfloat16)
    return result.reshape(rows.shape[0], rows.shape[1], -1)


def on_device(tokens, routes, probs, w_gate, w_up, w_down):
    groups = lax.axis_size("grp")
    shards = lax.axis_size("shard")
    per_group = shards // TPE
    experts_all = groups * per_group
    tok_count = tokens.shape[0]
    top_count = routes.shape[1]
    capacity = 2 * tok_count * top_count // experts_all
    local = lax.axis_index("shard") // TPE
    targets = jnp.arange(groups, dtype=jnp.int32) * per_group + local
    gates = probs / jnp.sum(probs, axis=-1, keepdims=True)
    match = routes[:, :, None] == targets[None, None, :]
    hits = jnp.sum(match.astype(jnp.int32), axis=1)
    gate_hits = jnp.sum(jnp.where(match, gates[:, :, None], jnp.float32(0.0)), axis=1)
    ranks = jnp.cumsum(hits, axis=0) - 1
    slots = jnp.arange(capacity, dtype=jnp.int32)
    select = ((hits.T[:, None, :] > 0) & (ranks.T[:, None, :] == slots[None, :, None])).astype(
        jnp.bfloat16
    )
    outgoing = jnp.einsum("gct,td->gcd", select, tokens, preferred_element_type=jnp.float32).astype(
        jnp.bfloat16
    )
    arrived = lax.all_to_all(outgoing, "grp", split_axis=0, concat_axis=0, tiled=True)
    results = tile_pass(arrived, w_gate, w_up, w_down)
    returned = lax.all_to_all(results, "grp", split_axis=0, concat_axis=0, tiled=True)

    def add_group(total, items):
        picks, rows_back, weight = items
        picked = jnp.einsum("ct,cd->td", picks, rows_back, preferred_element_type=jnp.float32)
        return (total + weight[:, None] * picked, None)

    start = jnp.zeros((tok_count, tokens.shape[1]), jnp.float32)
    combined, unused = lax.scan(add_group, start, (select, returned, gate_hits.T))
    return lax.psum_scatter(combined, "shard", scatter_dimension=1, tiled=True).astype(jnp.bfloat16)


def solution(mesh):
    return jax.shard_map(
        on_device,
        mesh=mesh,
        in_specs=(
            P(("grp", "side"), None),
            P(("grp", "side"), None),
            P(("grp", "side"), None),
            P(("grp", "shard"), None, None),
            P(("grp", "shard"), None, None),
            P(("grp", "shard"), None, None),
        ),
        out_specs=P(("grp", "side"), "shard"),
        check_vma=False,
    )
```

profile of v0, /device:TPU:0, one launch (start us, length us, event | category | flops | bytes accessed | tf_op | source)
XLA Modules:
  0.0 120.8 jit_solution(16905066792228107948)
XLA Ops:
  6.5 0.0 copy-start
  6.5 0.9 fusion.33
  7.4 0.1 copy.11
  7.6 0.1 reduce_window_sum.11
  7.7 0.1 copy.12
  7.7 1.7 %convolution_convert_fusion.1 = bf16[4,64,4096]{2,1,0:T(8,128)(2,1)S(1)} fusion(bf16[64,4096]{1,0:T(8,128)(2,1)} %param.8, s32[4,64]{1,0:T(4,128)S(1)} %copy.12, pred[4,64]{1,0:T(4,128)(4,1)S(1)} %compare_bitcast_fusion), kind=kOutput, calls=%fused_computation.10 | convolution fusion | flops 135299072 | bytes 2622720 | tf_op jit(solution)/shard_map/gct,td->gcd/dot_general | solution.py:37
  9.5 0.0 copy-start.3
  9.5 29.9 %all_to_all.10 = bf16[4,64,4096]{2,1,0:T(8,128)(2,1)S(1)} all-to-all(bf16[4,64,4096]{2,1,0:T(8,128)(2,1)S(1)} %convolution_convert_fusion.1), channel_id=1, replica_groups=mesh['grp'=4,'shard'=4,'side'=2] {'grp'}, dimensions={0} | all-to-all | bytes 4194304 | tf_op jit(solution)/shard_map/all_to_all | solution.py:40
  39.3 1.3 %copy-done.2 = bf16[4,64,4096]{2,1,0:T(8,128)(2,1)} copy-done((bf16[4,64,4096]{2,1,0:T(8,128)(2,1)}, bf16[4,64,4096]{2,1,0:T(8,128)(2,1)S(1)}, u32[]{:S(2)}) %copy-start.2) | copy-done | bytes 2097176
  40.7 0.7 fusion.10
  41.4 5.9 %convolution_convert_fusion = bf16[256,4096]{1,0:T(8,128)(2,1)} fusion(bf16[1,256,4096]{2,1,0:T(8,128)(2,1)S(1)} %copy-done, bf16[256,4096]{1,0:T(8,128)(2,1)} %bitcast.42, bf16[1,4096,256]{2,1,0:T(8,128)(2,1)} %param.12, f32[256,256]{1,0:T(8,128)S(1)} %fusion.10), kind=kOutput, calls=%fused_computation.9 | convolution fusion | flops 1075183616 | bytes 8650752 | tf_op jit(solution)/shard_map/dot_general | solution.py:14
  47.3 4.6 %all-to-all-start.1 = ((bf16[4,64,4096]{2,1,0:T(8,128)(2,1)}), bf16[4,64,4096]{2,1,0:T(8,128)(2,1)}, u32[]{:S(2)}, u32[]{:S(2)}) async-start(bf16[4,64,4096]{2,1,0:T(8,128)(2,1)} %bitcast.43), calls=%async_computation.1 | async-start | bytes 4194304 | tf_op jit(solution)/shard_map/all_to_all | solution.py:42
  51.9 0.0 reduce-scatter.2.cloned.1.call-start
  52.0 0.1 fusion.32
  52.1 25.5 %all-to-all-done.1 = bf16[4,64,4096]{2,1,0:T(8,128)(2,1)} async-done(((bf16[4,64,4096]{2,1,0:T(8,128)(2,1)}), bf16[4,64,4096]{2,1,0:T(8,128)(2,1)}, u32[]{:S(2)}, u32[]{:S(2)}) %all-to-all-start.1) | async-done | bytes 2097184 | tf_op jit(solution)/shard_map/all_to_all | solution.py:42
  77.7 6.1 %while.11 = (s32[]{:T(128)}, f32[64,4096]{1,0:T(8,128)S(1)}, f32[4,64]{1,0:T(4,128)S(1)}, bf16[4,64,64]{2,1,0:T(8,128)(2,1)S(1)}, bf16[4,64,4096]{2,1,0:T(8,128)(2,1)}, /*index=5*/s32[]{:T(128)}, s32[]{:T(128)}) while((s32[]{:T(128)}, f32[64,4096]{1,0:T(8,128)S(1)}, f32[4,64]{1,0:T(4,128)S(1)}, bf16[4,64,64]{2,1,0:T(8,128)(2,1)S(1)}, ...), condition=%wide.region_5.6_spmd.clone, body=%wide.region_4.5_spmd.clone.sunk | while | flops 34340864 | bytes 2639963 | solution.py:50
  77.7 1.5 %fusion.44 = f32[64,4096]{1,0:T(8,128)S(1)} fusion(f32[64,4096]{1,0:T(8,128)S(1)} %get-tuple-element.100, bf16[4,64,4096]{2,1,0:T(8,128)(2,1)} %get-tuple-element.110, s32[]{:T(128)} %get-tuple-element.99, f32[64]{0:T(128)S(1)} %fusion.43, pred[]{:T(512)S(6)} %compare.5, bf16[4,64,64]{2,1,0:T(8,128)(2,1)S(1)} %get-tuple-element.109), kind=kOutput, calls=%fused_computation.1.clone.1 | convolution fusion | flops 34340864 | bytes 2639361 | tf_op jit(solution)/shard_map/while/body/eval_jaxpr/ct,cd->td/dot_general | solution.py:46
  79.2 1.5 %fusion.44 = f32[64,4096]{1,0:T(8,128)S(1)} fusion(f32[64,4096]{1,0:T(8,128)S(1)} %get-tuple-element.100, bf16[4,64,4096]{2,1,0:T(8,128)(2,1)} %get-tuple-element.110, s32[]{:T(128)} %get-tuple-element.99, f32[64]{0:T(128)S(1)} %fusion.43, pred[]{:T(512)S(6)} %compare.5, bf16[4,64,64]{2,1,0:T(8,128)(2,1)S(1)} %get-tuple-element.109), kind=kOutput, calls=%fused_computation.1.clone.1 | convolution fusion | flops 34340864 | bytes 2639361 | tf_op jit(solution)/shard_map/while/body/eval_jaxpr/ct,cd->td/dot_general | solution.py:46
  80.7 1.5 %fusion.44 = f32[64,4096]{1,0:T(8,128)S(1)} fusion(f32[64,4096]{1,0:T(8,128)S(1)} %get-tuple-element.100, bf16[4,64,4096]{2,1,0:T(8,128)(2,1)} %get-tuple-element.110, s32[]{:T(128)} %get-tuple-element.99, f32[64]{0:T(128)S(1)} %fusion.43, pred[]{:T(512)S(6)} %compare.5, bf16[4,64,64]{2,1,0:T(8,128)(2,1)S(1)} %get-tuple-element.109), kind=kOutput, calls=%fused_computation.1.clone.1 | convolution fusion | flops 34340864 | bytes 2639361 | tf_op jit(solution)/shard_map/while/body/eval_jaxpr/ct,cd->td/dot_general | solution.py:46
  82.2 1.5 %fusion.44 = f32[64,4096]{1,0:T(8,128)S(1)} fusion(f32[64,4096]{1,0:T(8,128)S(1)} %get-tuple-element.100, bf16[4,64,4096]{2,1,0:T(8,128)(2,1)} %get-tuple-element.110, s32[]{:T(128)} %get-tuple-element.99, f32[64]{0:T(128)S(1)} %fusion.43, pred[]{:T(512)S(6)} %compare.5, bf16[4,64,64]{2,1,0:T(8,128)(2,1)S(1)} %get-tuple-element.109), kind=kOutput, calls=%fused_computation.1.clone.1 | convolution fusion | flops 34340864 | bytes 2639361 | tf_op jit(solution)/shard_map/while/body/eval_jaxpr/ct,cd->td/dot_general | solution.py:46
  83.7 1.0 copy-done.1
  84.7 0.0 reduce-scatter.2.cloned.1.call-update
  84.7 27.6 %reduce-scatter.2.cloned.1.call-done = f32[64,1024]{1,0:T(8,128)} async-done(((f32[64,4096]{1,0:T(8,128)}), f32[64,1024]{1,0:T(8,128)}) %reduce-scatter.2.cloned.1.call-update) | async-done | bytes 262160 | tf_op jit(solution)/shard_map/reduce_scatter | solution.py:51
  112.4 1.6 %convert_element_type.23 = bf16[64,1024]{1,0:T(8,128)(2,1)} convert(f32[64,1024]{1,0:T(8,128)} %reduce-scatter.2.cloned.1.call-done) | non-fusion elementwise | flops 65536 | bytes 393216 | tf_op jit(solution)/shard_map/convert_element_type | solution.py:51
  (19 shorter events, 0.1 us)
Async XLA Ops:
  6.5 34.9 %copy-start = (bf16[1,256,4096]{2,1,0:T(8,128)(2,1)S(1)}, bf16[1,256,4096]{2,1,0:T(8,128)(2,1)}, u32[]{:S(2)}) copy-start(bf16[1,256,4096]{2,1,0:T(8,128)(2,1)} %param.13) | copy-start | bytes 6291460
  9.5 31.2 %copy-start.3 = (bf16[1,4096,256]{2,1,0:T(8,128)(2,1)S(1)}, bf16[1,4096,256]{2,1,0:T(8,128)(2,1)}, u32[]{:S(2)}) copy-start(bf16[1,4096,256]{2,1,0:T(8,128)(2,1)} %param.11) | copy-start | bytes 6291460
  39.3 1.4 %copy-start.2 = (bf16[4,64,4096]{2,1,0:T(8,128)(2,1)}, bf16[4,64,4096]{2,1,0:T(8,128)(2,1)S(1)}, u32[]{:S(2)}) copy-start(bf16[4,64,4096]{2,1,0:T(8,128)(2,1)S(1)} %all_to_all.10) | copy-start | bytes 6291460
  47.3 4.6 %copy-start.4 = (f32[64,2]{0,1:T(2,128)S(1)}, f32[64,2]{0,1:T(2,128)}, u32[]{:S(2)}) copy-start(f32[64,2]{0,1:T(2,128)} %param.10) | copy-start | bytes 1540
  47.3 4.7 %copy-start.5 = (s32[64,2]{0,1:T(2,128)S(1)}, s32[64,2]{0,1:T(2,128)}, u32[]{:S(2)}) copy-start(s32[64,2]{0,1:T(2,128)} %param.9) | copy-start | bytes 1540
  47.3 30.3 %all-to-all-start.1 = ((bf16[4,64,4096]{2,1,0:T(8,128)(2,1)}), bf16[4,64,4096]{2,1,0:T(8,128)(2,1)}, u32[]{:S(2)}, u32[]{:S(2)}) async-start(bf16[4,64,4096]{2,1,0:T(8,128)(2,1)} %bitcast.43), calls=%async_computation.1 | async-start | bytes 4194304 | tf_op jit(solution)/shard_map/all_to_all | solution.py:42
  51.9 60.5 %reduce-scatter.2.cloned.1.call-start = ((), (), s32[]{:S(2)}) async-start(), calls=%async_computation.3 | async-start | bytes 1310720 | tf_op jit(solution)/shard_map/reduce_scatter | solution.py:51
  83.7 1.0 copy-start.1
Sparse Core Ops, SparseCore 0:
  84.9 27.4 reduce-scatter.1
where the time goes:
time: 121 us
  waiting for transfers between devices  53.2 us (44%)
  blocking collectives  29.9 us (25%)
  matrix products  14.3 us (12%)
  between operations  13.5 us (11%)
  starting transfers between devices  4.61 us (4%)
  other arithmetic  2.77 us (2%)
  local copies, waits for them, and re-layouts  2.55 us (2%)
    all_to_all x1, blocking collectives, on_device(): lax.all_to_all(outgoing, 'grp', split_axis=0, concat_axis=0, tiled=True)  29.9 us
    reduce_scatter x1, waiting for transfers between devices, on_device(): lax.psum_scatter(combined, 'shard', scatter_dimension=1, tiled=True)  27.6 us
    all_to_all x1, waiting for transfers between devices, on_device(): lax.all_to_all(results, 'grp', split_axis=0, concat_axis=0, tiled=True)  25.5 us
    dot_general x4, matrix products, add_group(): jnp.einsum('ct,cd->td', picks, rows_back, preferred_element_type=jnp.floa...  5.92 us
    dot_general x1, matrix products, tile_pass(): jnp.dot(hidden, w_down[0], preferred_element_type=jnp.float32)  5.89 us
    all_to_all x1, starting transfers between devices, on_device(): lax.all_to_all(results, 'grp', split_axis=0, concat_axis=0, tiled=True)  4.57 us
  transfers between devices with their start and end apart: 2, of which 2 were waited for; matrix products, arithmetic and copies ran while one was open for 0% of the time, Pallas kernels for 0%

commit v1 on v0

--- a/solution.py
+++ b/solution.py
@@ -1,9 +1,15 @@
+import functools
+
 import jax
 import jax.numpy as jnp
 from jax import lax
+from jax.experimental import pallas as pl
+from jax.experimental.pallas import tpu as pltpu
 from jax.sharding import PartitionSpec as P
 
 TPE = 4
+CHUNK = 16
+MESH = pl.DeviceIdType.MESH
 
 
 def tile_pass(rows, w_gate, w_up, w_down):
@@ -51,18 +57,250 @@
     return lax.psum_scatter(combined, "shard", scatter_dimension=1, tiled=True).astype(jnp.bfloat16)
 
 
+def dense_kernel(
+    groups, shards, tokens, routes, probs, wg_hbm, wu_hbm, wd_hbm, out,
+    x, gt, wg, wu, wd, own, cross, lend, borrowed, y_out, y_in, z_out, z_in, local_sem, send_sem, recv_sem,
+):
+    chunks, rows_per, width = tokens.shape
+    half = chunks // 2
+    rows = chunks * rows_per
+    depth = wg.shape[0]
+    grp, z = lax.axis_index("grp"), lax.axis_index("shard")
+    odd = lax.rem(z, 2)
+    sibling = {"grp": grp + 1 - 2 * lax.rem(grp, 2)}
+    over = lax.rem(grp + 2, groups)
+    across = {"grp": over}
+    diagonal = {"grp": over + 1 - 2 * lax.rem(over, 2)}
+    pair = {"shard": z + 1 - 2 * odd}
+    rest = [{"shard": lax.rem(z + d, shards)} for d in range(1, shards)]
+
+    loads = [
+        pltpu.make_async_copy(wg_hbm.at[0], wg, local_sem.at[0]),
+        pltpu.make_async_copy(wu_hbm.at[0], wu, local_sem.at[1]),
+        pltpu.make_async_copy(wd_hbm.at[0], wd, local_sem.at[2]),
+    ]
+    starts = [half * odd, half * (1 - odd)]
+    loads += [
+        pltpu.make_async_copy(tokens.at[pl.ds(starts[i], half)], x.at[0, pl.ds(i * half, half)], local_sem.at[3 + i])
+        for i in range(2)
+    ]
+    for load in loads:
+        load.start()
+
+    barrier = pltpu.get_barrier_semaphore()
+    greeted = [sibling, across, diagonal] + rest
+    for device in greeted:
+        pl.semaphore_signal(barrier, inc=1, device_id=device, device_id_type=MESH)
+
+    share = probs[...] / jnp.sum(probs[...], axis=1, keepdims=True)
+    row_at = lax.rem(lax.broadcasted_iota(jnp.int32, (rows, gt.shape[2]), 0) + half * rows_per * odd, rows)
+    diag = row_at == lax.broadcasted_iota(jnp.int32, (rows, gt.shape[2]), 1)
+    gt[0] = jnp.zeros(gt.shape[1:], jnp.float32)
+    for expert in range(groups):
+        column = jnp.sum(jnp.where(routes[...] == expert, share, 0.0), axis=1, keepdims=True)
+        gt[0, expert : expert + 1, :] = jnp.sum(jnp.where(diag, column, 0.0), axis=0, keepdims=True)
+
+    pl.semaphore_wait(barrier, len(greeted))
+
+    number = [0]
+
+    def remote(from_ref, to_ref, device):
+        at = number[0]
+        number[0] += 1
+        return pltpu.make_async_remote_copy(
+            src_ref=from_ref, dst_ref=to_ref, send_sem=send_sem.at[at], recv_sem=recv_sem.at[at],
+            device_id=device, device_id_type=MESH,
+        )
+
+    sent = []
+
+    def begin(copy):
+        copy.start()
+        sent.append(copy)
+        return copy
+
+    direct = [begin(remote(tokens.at[half * odd + k], x.at[2, k], across)) for k in range(half)]
+    beside = [
+        begin(remote(tokens.at[pl.ds(starts[i], half)], x.at[1, pl.ds(i * half, half)], sibling)) for i in range(2)
+    ]
+    gate_copies = [
+        begin(remote(gt.at[0], gt.at[slot], device))
+        for slot, device in ((1, sibling), (2, across), (3, diagonal))
+    ]
+    paired = [remote(x.at[2, k], x.at[2, half + k], pair) for k in range(half)]
+    passed = [remote(x.at[2, k], x.at[3, k], sibling) for k in range(chunks)]
+    lent_home = remote(lend.at[0], borrowed.at[0], sibling)
+    lent_away = [
+        remote(lend.at[1, pl.ds(i * half, half)], borrowed.at[1, pl.ds(i * half, half)], sibling) for i in range(2)
+    ]
+    y_copies = [remote(y_out.at[r], y_in.at[r], across) for r in range(chunks)]
+    z_base = number[0]
+
+    def z_copy(step, r, to_index):
+        return pltpu.make_async_remote_copy(
+            src_ref=z_out.at[r, lax.rem(z + step, shards)],
+            dst_ref=z_in.at[step - 1, to_index],
+            send_sem=send_sem.at[z_base + (step - 1) * chunks + r],
+            recv_sem=recv_sem.at[z_base + (step - 1) * chunks + to_index],
+            device_id=rest[step - 1],
+            device_id_type=MESH,
+        )
+
+    def gate_column(slot, first, count):
+        picked = jnp.where(lax.broadcasted_iota(jnp.int32, gt.shape[1:], 0) == grp, gt[slot], 0.0)
+        line = jnp.sum(picked, axis=0, keepdims=True)
+        at = lax.broadcasted_iota(jnp.int32, (count, gt.shape[2]), 0) + first
+        return jnp.sum(
+            jnp.where(at == lax.broadcasted_iota(jnp.int32, (count, gt.shape[2]), 1), line, 0.0), axis=1, keepdims=True
+        )
+
+    def experts(slot, first, count, kept, given):
+        each = count * rows_per
+        steps = 4
+        span = depth // steps
+        gate = jnp.zeros((2 * each, wg.shape[1]), jnp.float32)
+        upper = jnp.zeros((2 * each, wg.shape[1]), jnp.float32)
+        for step in range(steps):
+            piece = x[slot : slot + 2, first : first + count, :, step * span : (step + 1) * span]
+            piece = piece.reshape(2 * each, span)
+            gate += jnp.dot(piece, wg[step * span : (step + 1) * span, :], preferred_element_type=jnp.float32)
+            upper += jnp.dot(piece, wu[step * span : (step + 1) * span, :], preferred_element_type=jnp.float32)
+        hidden = (gate / (1.0 + jnp.exp(-gate)) * upper).astype(jnp.bfloat16)
+        scale = jnp.concatenate(
+            [gate_column(slot, first * rows_per, each), gate_column(slot + 1, first * rows_per, each)], axis=0
+        )
+        cw = width // shards
+        for q in range(shards):
+            part = jnp.dot(hidden, wd[:, q * cw : (q + 1) * cw], preferred_element_type=jnp.float32) * scale
+            kept[first : first + count, q] = part[:each].reshape(count, rows_per, cw)
+            lend[given, first : first + count, q] = part[each:].astype(jnp.bfloat16).reshape(count, rows_per, cw)
+
+    def arrive(k):
+        direct[k].wait_recv()
+        begin(paired[k])
+        begin(passed[k])
+
+    def arrive_pair(k):
+        paired[k].wait_recv()
+        begin(passed[half + k])
+
+    def to_across(part):
+        lent_away[part].wait_recv()
+        for r in range(part * half, (part + 1) * half):
+            y_out[r] = (cross[r] + borrowed[1, r].astype(jnp.float32)).astype(jnp.bfloat16)
+            begin(y_copies[r])
+
+    for k in range(half - 1):
+        arrive(k)
+    for load in loads:
+        load.wait()
+    for copy in beside + gate_copies:
+        copy.wait_recv()
+    experts(0, 0, chunks, own, 0)
+    begin(lent_home)
+    arrive(half - 1)
+    for k in range(half - 1):
+        arrive_pair(k)
+    for r in range(half):
+        passed[r].wait_recv()
+    experts(2, 0, half, cross, 1)
+    begin(lent_away[0])
+    arrive_pair(half - 1)
+    to_across(0)
+    for r in range(half, chunks):
+        passed[r].wait_recv()
+    experts(2, half, half, cross, 1)
+    begin(lent_away[1])
+    to_across(1)
+
+    lent_home.wait_recv()
+    for r in range(chunks):
+        y_copies[r].wait_recv()
+        total = own[r] + borrowed[0, r].astype(jnp.float32) + y_in[r].astype(jnp.float32)
+        own[r] = total
+        z_out[r] = total.astype(jnp.bfloat16)
+        for step in range(1, shards):
+            begin(z_copy(step, r, lax.rem(r + half * lax.rem(step, 2), chunks)))
+    for r in range(chunks):
+        total = own[r, z]
+        for step in range(1, shards):
+            z_copy(step, r, r).wait_recv()
+            total = total + z_in[step - 1, r].astype(jnp.float32)
+        out[lax.rem(r + half * odd, chunks)] = total.astype(jnp.bfloat16)
+    for copy in sent:
+        copy.wait_send()
+
+
+def dense_on_device(tokens, routes, probs, w_gate, w_up, w_down):
+    groups, shards = lax.axis_size("grp"), lax.axis_size("shard")
+    tok_count, width = tokens.shape
+    depth, tile = w_gate.shape[1:]
+    chunks, cw = tok_count // CHUNK, width // shards
+    half = chunks // 2
+    copies = half + 2 + 3 + half + chunks + 1 + 2 + chunks + (shards - 1) * chunks
+    lanes = -(-tok_count // 128) * 128
+    bf16, f32 = jnp.bfloat16, jnp.float32
+    block = (chunks, shards, CHUNK, cw)
+    whole = pl.BlockSpec(memory_space=pltpu.VMEM)
+    away = pl.BlockSpec(memory_space=pl.ANY)
+    total_rows = groups * tok_count
+    mixed = pl.pallas_call(
+        functools.partial(dense_kernel, groups, shards),
+        out_shape=jax.ShapeDtypeStruct((chunks, CHUNK, cw), bf16),
+        in_specs=[away, whole, whole, away, away, away],
+        out_specs=whole,
+        scratch_shapes=[
+            pltpu.VMEM((4, chunks, CHUNK, width), bf16),
+            pltpu.VMEM((4, -(-groups // 8) * 8, lanes), f32),
+            pltpu.VMEM((depth, tile), bf16),
+            pltpu.VMEM((depth, tile), bf16),
+            pltpu.VMEM((tile, width), bf16),
+            pltpu.VMEM(block, f32),
+            pltpu.VMEM(block, f32),
+            pltpu.VMEM((2,) + block, bf16),
+            pltpu.VMEM((2,) + block, bf16),
+            pltpu.VMEM(block, bf16),
+            pltpu.VMEM(block, bf16),
+            pltpu.VMEM(block, bf16),
+            pltpu.VMEM((shards - 1, chunks, CHUNK, cw), bf16),
+            pltpu.SemaphoreType.DMA((5,)),
+            pltpu.SemaphoreType.DMA((copies,)),
+            pltpu.SemaphoreType.DMA((copies,)),
+        ],
+        compiler_params=pltpu.CompilerParams(
+            collective_id=0, has_side_effects=True, vmem_limit_bytes=40 * 1024 * 1024
+        ),
+        cost_estimate=pl.CostEstimate(
+            flops=6 * total_rows * depth * tile, bytes_accessed=6 * depth * tile, transcendentals=total_rows * tile
+        ),
+    )(tokens.reshape(chunks, CHUNK, width), routes, probs, w_gate, w_up, w_down)
+    return mixed.reshape(tok_count, cw)
+
+
+def is_dense(mesh, tokens, routes):
+    groups, shards, sides = mesh.shape["grp"], mesh.shape["shard"], mesh.shape["side"]
+    tok_count = tokens.shape[0] // (groups * sides)
+    per_group = shards // TPE
+    capacity = 2 * tok_count * routes.shape[1] // (groups * per_group)
+    return groups == 4 and per_group == 1 and capacity >= tok_count and tok_count % (2 * CHUNK) == 0
+
+
 def solution(mesh):
-    return jax.shard_map(
-        on_device,
-        mesh=mesh,
-        in_specs=(
-            P(("grp", "side"), None),
-            P(("grp", "side"), None),
-            P(("grp", "side"), None),
-            P(("grp", "shard"), None, None),
-            P(("grp", "shard"), None, None),
-            P(("grp", "shard"), None, None),
-        ),
-        out_specs=P(("grp", "side"), "shard"),
-        check_vma=False,
-    )
+    def call(tokens, routes, probs, w_gate, w_up, w_down):
+        body = dense_on_device if is_dense(mesh, tokens, routes) else on_device
+        return jax.shard_map(
+            body,
+            mesh=mesh,
+            in_specs=(
+                P(("grp", "side"), None),
+                P(("grp", "side"), None),
+                P(("grp", "side"), None),
+                P(("grp", "shard"), None, None),
+                P(("grp", "shard"), None, None),
+                P(("grp", "shard"), None, None),
+            ),
+            out_specs=P(("grp", "side"), "shard"),
+            check_vma=False,
+        )(tokens, routes, probs, w_gate, w_up, w_down)
+
+    return call

time: 121 us -> 45.7 us (0.38)
  waiting for transfers between devices: 53.2 us -> 0 us
  Pallas kernels: 0 us -> 37.4 us
  blocking collectives: 29.9 us -> 0 us
  matrix products: 14.3 us -> 0 us
  between operations: 13.5 us -> 0.01 us
  local copies, waits for them, and re-layouts: 2.55 us -> 8.01 us
  starting transfers between devices: 4.61 us -> 0 us
  other arithmetic: 2.77 us -> 0 us
    pallas_call x0 -> x1, Pallas kernels: none -> 37.4 us  [dense_on_device(): pl.pallas_call(functools.partial(dense_kernel, groups, shards), out_shape...]
    all_to_all x1 -> x0, blocking collectives: 29.9 us -> none  [on_device(): lax.all_to_all(outgoing, 'grp', split_axis=0, concat_axis=0, tiled=True)]
    reduce_scatter x1 -> x0, waiting for transfers between devices: 27.6 us -> none  [on_device(): lax.psum_scatter(combined, 'shard', scatter_dimension=1, tiled=True)]
    all_to_all x1 -> x0, waiting for transfers between devices: 25.5 us -> none  [on_device(): lax.all_to_all(results, 'grp', split_axis=0, concat_axis=0, tiled=True)]
    dot_general x7 -> x0, matrix products: 14.3 us -> none  [the longest x4 5.92 us: add_group(): jnp.einsum('ct,cd->td', picks, rows_back, preferred_element_type=jnp.floa...]
    unnamed x12 -> x11, local copies, waits for them, and re-layouts: 2.35 us -> 8.01 us
    all_to_all x1 -> x0, starting transfers between devices: 4.57 us -> none  [on_device(): lax.all_to_all(results, 'grp', split_axis=0, concat_axis=0, tiled=True)]
    convert_element_type x2 -> x0, other arithmetic: 1.65 us -> none  [the longest x1 1.62 us: on_device(): lax.psum_scatter(combined, 'shard', scatter_dimension=1, tiled=True)]
  transfers between devices with their start and end apart: 2 -> 0, of which waited for: 2 -> 0; matrix products, arithmetic and copies ran while one was open for 0% -> 0% of each run, Pallas kernels for 0% -> 0%
where the time goes in v1:
time: 45.7 us; the launch traced here: 45.4 us
  Pallas kernels  37.4 us (82%)
  local copies, waits for them, and re-layouts  8.01 us (18%)
    pallas_call x1, Pallas kernels, dense_on_device(): pl.pallas_call(functools.partial(dense_kernel, groups, shards), out_shape...  37.4 us
    unnamed x11, local copies, waits for them, and re-layouts  8.01 us

profile of v1, /device:TPU:0, one launch (start us, length us, event | category | flops | bytes accessed | tf_op | source)
XLA Modules:
  0.0 45.4 jit_solution(15421989855302666247)
XLA Ops:
  0.0 0.8 %copy.7.routes = s32[64,2]{1,0:T(8,128)S(1)} copy(s32[64,2]{0,1:T(2,128)} %param.7) | data formatting | bytes 1024 | tf_op args[1]
  0.8 0.8 %copy.8.probs = f32[64,2]{1,0:T(8,128)S(1)} copy(f32[64,2]{0,1:T(2,128)} %param.8) | data formatting | bytes 1024 | tf_op args[2]
  1.5 0.0 copy-start
  1.5 1.6 %copy-done = bf16[1,4096,256]{2,1,0:T(8,128)(2,1)S(1)} copy-done((bf16[1,4096,256]{2,1,0:T(8,128)(2,1)S(1)}, bf16[1,4096,256]{2,1,0:T(8,128)(2,1)}, u32[]{:S(2)}) %copy-start) | copy-done | bytes 2097176
  3.1 0.0 copy-start.1
  3.1 1.6 %copy-done.1 = bf16[1,4096,256]{2,1,0:T(8,128)(2,1)S(1)} copy-done((bf16[1,4096,256]{2,1,0:T(8,128)(2,1)S(1)}, bf16[1,4096,256]{2,1,0:T(8,128)(2,1)}, u32[]{:S(2)}) %copy-start.1) | copy-done | bytes 2097176
  4.7 0.0 copy-start.2
  4.7 1.6 %copy-done.2 = bf16[1,256,4096]{2,1,0:T(8,128)(2,1)S(1)} copy-done((bf16[1,256,4096]{2,1,0:T(8,128)(2,1)S(1)}, bf16[1,256,4096]{2,1,0:T(8,128)(2,1)}, u32[]{:S(2)}) %copy-start.2) | copy-done | bytes 2097176
  6.3 0.0 copy-start.3
  6.3 1.0 %copy-done.3 = bf16[64,4096]{1,0:T(8,128)(2,1)S(1)} copy-done((bf16[64,4096]{1,0:T(8,128)(2,1)S(1)}, bf16[64,4096]{1,0:T(8,128)(2,1)}, u32[]{:S(2)}) %copy-start.3) | copy-done | bytes 524312
  7.4 37.4 %shard_map.64 = bf16[4,16,1024]{2,1,0:T(8,128)(2,1)S(1)} custom-call(bf16[4,16,4096]{2,1,0:T(8,128)(2,1)S(1)} %bitcast.3, s32[64,2]{1,0:T(8,128)S(1)} %copy.7.routes, f32[64,2]{1,0:T(8,128)S(1)} %copy.8.probs, bf16[1,4096,256]{2,1,0:T(8,128)(2,1)S(1)} %copy-done, bf16[1,4096,256]{2,1,0:T(8,128)(2,1)S(1)} %copy-done.1, bf16[1,256,4096]{2,1,0:T(8,128)(2,1)S(1)} %copy-done.2), custom_call_target="tpu_custom_call" | custom-call | flops 1610612736 | bytes 6291456 | tf_op jit(solution)/shard_map/pallas_call | solution.py:247
  44.8 0.7 %copy.10 = bf16[64,1024]{1,0:T(8,128)(2,1)} copy(bf16[64,1024]{1,0:T(8,128)(2,1)S(1)} %bitcast.2) | data formatting | bytes 262144
Async XLA Ops:
  1.5 1.6 %copy-start = (bf16[1,4096,256]{2,1,0:T(8,128)(2,1)S(1)}, bf16[1,4096,256]{2,1,0:T(8,128)(2,1)}, u32[]{:S(2)}) copy-start(bf16[1,4096,256]{2,1,0:T(8,128)(2,1)} %wg_hbm.1) | copy-start | bytes 6291460
  3.1 1.6 %copy-start.1 = (bf16[1,4096,256]{2,1,0:T(8,128)(2,1)S(1)}, bf16[1,4096,256]{2,1,0:T(8,128)(2,1)}, u32[]{:S(2)}) copy-start(bf16[1,4096,256]{2,1,0:T(8,128)(2,1)} %wu_hbm.1) | copy-start | bytes 6291460
  4.7 1.6 %copy-start.2 = (bf16[1,256,4096]{2,1,0:T(8,128)(2,1)S(1)}, bf16[1,256,4096]{2,1,0:T(8,128)(2,1)}, u32[]{:S(2)}) copy-start(bf16[1,256,4096]{2,1,0:T(8,128)(2,1)} %wd_hbm.1) | copy-start | bytes 6291460
  6.3 1.0 %copy-start.3 = (bf16[64,4096]{1,0:T(8,128)(2,1)S(1)}, bf16[64,4096]{1,0:T(8,128)(2,1)}, u32[]{:S(2)}) copy-start(bf16[64,4096]{1,0:T(8,128)(2,1)} %param.6) | copy-start | bytes 1572868

commit v2 on v1

--- a/solution.py
+++ b/solution.py
@@ -92,13 +92,11 @@
     for device in greeted:
         pl.semaphore_signal(barrier, inc=1, device_id=device, device_id_type=MESH)
 
-    share = probs[...] / jnp.sum(probs[...], axis=1, keepdims=True)
-    row_at = lax.rem(lax.broadcasted_iota(jnp.int32, (rows, gt.shape[2]), 0) + half * rows_per * odd, rows)
-    diag = row_at == lax.broadcasted_iota(jnp.int32, (rows, gt.shape[2]), 1)
+    share = probs[...] / jnp.sum(probs[...], axis=0, keepdims=True)
     gt[0] = jnp.zeros(gt.shape[1:], jnp.float32)
     for expert in range(groups):
-        column = jnp.sum(jnp.where(routes[...] == expert, share, 0.0), axis=1, keepdims=True)
-        gt[0, expert : expert + 1, :] = jnp.sum(jnp.where(diag, column, 0.0), axis=0, keepdims=True)
+        line = jnp.sum(jnp.where(routes[...] == expert, share, 0.0), axis=0, keepdims=True)
+        gt[0, expert : expert + 1, 0:rows] = line
 
     pl.semaphore_wait(barrier, len(greeted))
 
@@ -149,7 +147,8 @@
     def gate_column(slot, first, count):
         picked = jnp.where(lax.broadcasted_iota(jnp.int32, gt.shape[1:], 0) == grp, gt[slot], 0.0)
         line = jnp.sum(picked, axis=0, keepdims=True)
-        at = lax.broadcasted_iota(jnp.int32, (count, gt.shape[2]), 0) + first
+        at = lax.broadcasted_iota(jnp.int32, (count, gt.shape[2]), 0) + (first + half * rows_per * odd)
+        at = lax.rem(at, rows)
         return jnp.sum(
             jnp.where(at == lax.broadcasted_iota(jnp.int32, (count, gt.shape[2]), 1), line, 0.0), axis=1, keepdims=True
         )
@@ -242,7 +241,7 @@
     bf16, f32 = jnp.bfloat16, jnp.float32
     block = (chunks, shards, CHUNK, cw)
     whole = pl.BlockSpec(memory_space=pltpu.VMEM)
-    away = pl.BlockSpec(memory_space=pl.ANY)
+    away = pl.BlockSpec(memory_space=pltpu.HBM)
     total_rows = groups * tok_count
     mixed = pl.pallas_call(
         functools.partial(dense_kernel, groups, shards),
@@ -268,12 +267,12 @@
             pltpu.SemaphoreType.DMA((copies,)),
         ],
         compiler_params=pltpu.CompilerParams(
-            collective_id=0, has_side_effects=True, vmem_limit_bytes=40 * 1024 * 1024
+            collective_id=0, has_side_effects=True, vmem_limit_bytes=60 * 1024 * 1024
         ),
         cost_estimate=pl.CostEstimate(
             flops=6 * total_rows * depth * tile, bytes_accessed=6 * depth * tile, transcendentals=total_rows * tile
         ),
-    )(tokens.reshape(chunks, CHUNK, width), routes, probs, w_gate, w_up, w_down)
+    )(tokens.reshape(chunks, CHUNK, width), routes.T, probs.T, w_gate, w_up, w_down)
     return mixed.reshape(tok_count, cw)
 
 

time: 45.7 us -> 40.2 us (0.88)
  local copies, waits for them, and re-layouts: 8.01 us -> 1.57 us
  Pallas kernels: 37.4 us -> 38.5 us
    unnamed x11 -> x1, local copies, waits for them, and re-layouts: 8.01 us -> 1.57 us
    pallas_call x1, Pallas kernels: 37.4 us -> 38.5 us  [dense_on_device(): pl.pallas_call(functools.partial(dense_kernel, groups, shards), out_shape...]
where the time goes in v2:
time: 40.2 us; the launch traced here: 40.1 us
  Pallas kernels  38.5 us (96%)
  local copies, waits for them, and re-layouts  1.57 us (4%)
    pallas_call x1, Pallas kernels, dense_on_device(): pl.pallas_call(functools.partial(dense_kernel, groups, shards), out_shape...  38.5 us
    unnamed x1, local copies, waits for them, and re-layouts  1.57 us

profile of v2, /device:TPU:0, one launch (start us, length us, event | category | flops | bytes accessed | tf_op | source)
XLA Modules:
  0.0 40.1 jit_solution(4184360585794048532)
XLA Ops:
  0.0 38.5 %shard_map.64 = bf16[4,16,1024]{2,1,0:T(8,128)(2,1)} custom-call(bf16[4,16,4096]{2,1,0:T(8,128)(2,1)} %bitcast.4, s32[2,64]{1,0:T(2,128)} %bitcast.6, f32[2,64]{1,0:T(2,128)} %bitcast.7, bf16[1,4096,256]{2,1,0:T(8,128)(2,1)} %wg_hbm.1, bf16[1,4096,256]{2,1,0:T(8,128)(2,1)} %wu_hbm.1, bf16[1,256,4096]{2,1,0:T(8,128)(2,1)} %wd_hbm.1), custom_call_target="tpu_custom_call" | custom-call | flops 1610612736 | bytes 6291456 | tf_op jit(solution)/shard_map/pallas_call | solution.py:246
  38.5 1.6 %copy.8 = bf16[64,1024]{1,0:T(8,128)(2,1)} copy(bf16[64,1024]{1,0:T(8,128)(2,1)} %bitcast.5) | data formatting | bytes 262144

commit v3 on v2

--- a/solution.py
+++ b/solution.py
@@ -9,6 +9,7 @@
 
 TPE = 4
 CHUNK = 16
+PIECES = 2
 MESH = pl.DeviceIdType.MESH
 
 
@@ -117,7 +118,15 @@
         sent.append(copy)
         return copy
 
-    direct = [begin(remote(tokens.at[half * odd + k], x.at[2, k], across)) for k in range(half)]
+    wide = width // PIECES
+    spots = [(k, s) for k in range(half) for s in range(PIECES)]
+
+    def spot(ref, lead, k, s):
+        return ref.at[lead + (k, slice(None), pl.ds(s * wide, wide))]
+
+    direct = {
+        (k, s): begin(remote(spot(tokens, (), half * odd + k, s), spot(x, (2,), k, s), across)) for k, s in spots
+    }
     beside = [
         begin(remote(tokens.at[pl.ds(starts[i], half)], x.at[1, pl.ds(i * half, half)], sibling)) for i in range(2)
     ]
@@ -125,21 +134,21 @@
         begin(remote(gt.at[0], gt.at[slot], device))
         for slot, device in ((1, sibling), (2, across), (3, diagonal))
     ]
-    paired = [remote(x.at[2, k], x.at[2, half + k], pair) for k in range(half)]
-    passed = [remote(x.at[2, k], x.at[3, k], sibling) for k in range(chunks)]
+    paired = {(k, s): remote(spot(x, (2,), k, s), spot(x, (2,), half + k, s), pair) for k, s in spots}
+    every = [(r, s) for r in range(chunks) for s in range(PIECES)]
+    passed = {(r, s): remote(spot(x, (2,), r, s), spot(x, (3,), r, s), sibling) for r, s in every}
     lent_home = remote(lend.at[0], borrowed.at[0], sibling)
-    lent_away = [
-        remote(lend.at[1, pl.ds(i * half, half)], borrowed.at[1, pl.ds(i * half, half)], sibling) for i in range(2)
-    ]
-    y_copies = [remote(y_out.at[r], y_in.at[r], across) for r in range(chunks)]
+    lent_away = {(r, s): remote(lend.at[1, r, s], borrowed.at[1, r, s], sibling) for r, s in every}
+    y_copies = {(r, s): remote(y_out.at[r, s], y_in.at[r, s], across) for r, s in every}
     z_base = number[0]
 
-    def z_copy(step, r, to_index):
+    def z_copy(step, r, s, to_index):
+        row = z_base + ((step - 1) * PIECES + s) * chunks
         return pltpu.make_async_remote_copy(
-            src_ref=z_out.at[r, lax.rem(z + step, shards)],
-            dst_ref=z_in.at[step - 1, to_index],
-            send_sem=send_sem.at[z_base + (step - 1) * chunks + r],
-            recv_sem=recv_sem.at[z_base + (step - 1) * chunks + to_index],
+            src_ref=z_out.at[r, s, lax.rem(z + step, shards)],
+            dst_ref=z_in.at[step - 1, to_index, s],
+            send_sem=send_sem.at[row + r],
+            recv_sem=recv_sem.at[row + to_index],
             device_id=rest[step - 1],
             device_id_type=MESH,
         )
@@ -153,7 +162,7 @@
             jnp.where(at == lax.broadcasted_iota(jnp.int32, (count, gt.shape[2]), 1), line, 0.0), axis=1, keepdims=True
         )
 
-    def experts(slot, first, count, kept, given):
+    def enter(slot, first, count):
         each = count * rows_per
         steps = 4
         span = depth // steps
@@ -168,64 +177,87 @@
         scale = jnp.concatenate(
             [gate_column(slot, first * rows_per, each), gate_column(slot + 1, first * rows_per, each)], axis=0
         )
-        cw = width // shards
+        return hidden, scale
+
+    cw = width // shards
+    cs = cw // PIECES
+
+    def leave(entered, first, count, s, kept, given):
+        hidden, scale = entered
+        each = count * rows_per
         for q in range(shards):
-            part = jnp.dot(hidden, wd[:, q * cw : (q + 1) * cw], preferred_element_type=jnp.float32) * scale
-            kept[first : first + count, q] = part[:each].reshape(count, rows_per, cw)
-            lend[given, first : first + count, q] = part[each:].astype(jnp.bfloat16).reshape(count, rows_per, cw)
-
-    def arrive(k):
-        direct[k].wait_recv()
-        begin(paired[k])
-        begin(passed[k])
-
-    def arrive_pair(k):
-        paired[k].wait_recv()
-        begin(passed[half + k])
-
-    def to_across(part):
-        lent_away[part].wait_recv()
-        for r in range(part * half, (part + 1) * half):
-            y_out[r] = (cross[r] + borrowed[1, r].astype(jnp.float32)).astype(jnp.bfloat16)
-            begin(y_copies[r])
-
-    for k in range(half - 1):
-        arrive(k)
-    for load in loads:
-        load.wait()
+            at = q * cw + s * cs
+            part = jnp.dot(hidden, wd[:, at : at + cs], preferred_element_type=jnp.float32) * scale
+            kept[first : first + count, s, q] = part[:each].reshape(count, rows_per, cs)
+            lend[given, first : first + count, s, q] = part[each:].astype(jnp.bfloat16).reshape(count, rows_per, cs)
+
+    def arrive(k, s):
+        direct[k, s].wait_recv()
+        begin(paired[k, s])
+        begin(passed[k, s])
+
+    def arrive_pair(k, s):
+        paired[k, s].wait_recv()
+        begin(passed[half + k, s])
+
+    def to_across(r, s):
+        lent_away[r, s].wait_recv()
+        y_out[r, s] = (cross[r, s] + borrowed[1, r, s].astype(jnp.float32)).astype(jnp.bfloat16)
+        begin(y_copies[r, s])
+
+    def settle(r, s):
+        y_copies[r, s].wait_recv()
+        total = own[r, s] + borrowed[0, r, s].astype(jnp.float32) + y_in[r, s].astype(jnp.float32)
+        own[r, s] = total
+        z_out[r, s] = total.astype(jnp.bfloat16)
+        for step in range(1, shards):
+            begin(z_copy(step, r, s, lax.rem(r + half * lax.rem(step, 2), chunks)))
+
+    pieces = range(PIECES)
+    for i in (3, 4, 0, 1):
+        loads[i].wait()
     for copy in beside + gate_copies:
         copy.wait_recv()
-    experts(0, 0, chunks, own, 0)
+    entered = enter(0, 0, chunks)
+    for s in pieces:
+        arrive(0, s)
+    loads[2].wait()
+    for s in pieces:
+        leave(entered, 0, chunks, s, own, 0)
     begin(lent_home)
-    arrive(half - 1)
-    for k in range(half - 1):
-        arrive_pair(k)
-    for r in range(half):
-        passed[r].wait_recv()
-    experts(2, 0, half, cross, 1)
-    begin(lent_away[0])
-    arrive_pair(half - 1)
-    to_across(0)
-    for r in range(half, chunks):
-        passed[r].wait_recv()
-    experts(2, half, half, cross, 1)
-    begin(lent_away[1])
-    to_across(1)
-
+    waiting = [(k, s) for k in range(1, half) for s in pieces]
+    later = [(k, s) for k in range(half) for s in pieces]
+    settled = list(every)
+    for r in range(chunks):
+        if r < half:
+            for k, s in [spot_ for spot_ in waiting if spot_[0] == r]:
+                arrive(k, s)
+        else:
+            for k, s in [spot_ for spot_ in later if spot_[0] == r - half]:
+                arrive_pair(k, s)
+        for s in pieces:
+            passed[r, s].wait_recv()
+        entered = enter(2, r, 1)
+        if r > 0:
+            for s in pieces:
+                to_across(r - 1, s)
+        for s in pieces:
+            leave(entered, r, 1, s, cross, 1)
+            begin(lent_away[r, s])
     lent_home.wait_recv()
+    first_settled = settled.pop(0)
+    settle(*first_settled)
+    for s in pieces:
+        to_across(chunks - 1, s)
+    for r, s in settled:
+        settle(r, s)
     for r in range(chunks):
-        y_copies[r].wait_recv()
-        total = own[r] + borrowed[0, r].astype(jnp.float32) + y_in[r].astype(jnp.float32)
-        own[r] = total
-        z_out[r] = total.astype(jnp.bfloat16)
-        for step in range(1, shards):
-            begin(z_copy(step, r, lax.rem(r + half * lax.rem(step, 2), chunks)))
-    for r in range(chunks):
-        total = own[r, z]
-        for step in range(1, shards):
-            z_copy(step, r, r).wait_recv()
-            total = total + z_in[step - 1, r].astype(jnp.float32)
-        out[lax.rem(r + half * odd, chunks)] = total.astype(jnp.bfloat16)
+        for s in pieces:
+            total = own[r, s, z]
+            for step in range(1, shards):
+                z_copy(step, r, s, r).wait_recv()
+                total = total + z_in[step - 1, r, s].astype(jnp.float32)
+            out[lax.rem(r + half * odd, chunks), :, s * cs : (s + 1) * cs] = total.astype(jnp.bfloat16)
     for copy in sent:
         copy.wait_send()
 
@@ -236,10 +268,10 @@
     depth, tile = w_gate.shape[1:]
     chunks, cw = tok_count // CHUNK, width // shards
     half = chunks // 2
-    copies = half + 2 + 3 + half + chunks + 1 + 2 + chunks + (shards - 1) * chunks
+    copies = 2 + 3 + 1 + (2 * half + (3 + shards - 1) * chunks) * PIECES
     lanes = -(-tok_count // 128) * 128
     bf16, f32 = jnp.bfloat16, jnp.float32
-    block = (chunks, shards, CHUNK, cw)
+    block = (chunks, PIECES, shards, CHUNK, cw // PIECES)
     whole = pl.BlockSpec(memory_space=pltpu.VMEM)
     away = pl.BlockSpec(memory_space=pltpu.HBM)
     total_rows = groups * tok_count
@@ -261,13 +293,13 @@
             pltpu.VMEM(block, bf16),
             pltpu.VMEM(block, bf16),
             pltpu.VMEM(block, bf16),
-            pltpu.VMEM((shards - 1, chunks, CHUNK, cw), bf16),
+            pltpu.VMEM((shards - 1, chunks, PIECES, CHUNK, cw // PIECES), bf16),
             pltpu.SemaphoreType.DMA((5,)),
             pltpu.SemaphoreType.DMA((copies,)),
             pltpu.SemaphoreType.DMA((copies,)),
         ],
         compiler_params=pltpu.CompilerParams(
-            collective_id=0, has_side_effects=True, vmem_limit_bytes=60 * 1024 * 1024
+            collective_id=0, has_side_effects=True, vmem_limit_bytes=40 * 1024 * 1024
         ),
         cost_estimate=pl.CostEstimate(
             flops=6 * total_rows * depth * tile, bytes_accessed=6 * depth * tile, transcendentals=total_rows * tile
@@ -281,7 +313,7 @@
     tok_count = tokens.shape[0] // (groups * sides)
     per_group = shards // TPE
     capacity = 2 * tok_count * routes.shape[1] // (groups * per_group)
-    return groups == 4 and per_group == 1 and capacity >= tok_count and tok_count % (2 * CHUNK) == 0
+    return groups == 4 and per_group == 1 and capacity >= tok_count and tok_count % (2 * CHUNK) == 0 and tokens.shape[1] % (shards * PIECES * 128) == 0
 
 
 def solution(mesh):

time: 40.2 us -> 46.5 us (1.16)
  local copies, waits for them, and re-layouts: 1.57 us -> 7.83 us
    unnamed x1 -> x13, local copies, waits for them, and re-layouts: 1.57 us -> 7.83 us
where the time goes in v3:
time: 46.5 us; the launch traced here: 46.2 us
  Pallas kernels  38.3 us (82%)
  local copies, waits for them, and re-layouts  7.83 us (17%)
    pallas_call x1, Pallas kernels, dense_on_device(): pl.pallas_call(functools.partial(dense_kernel, groups, shards), out_shape...  38.3 us
    unnamed x13, local copies, waits for them, and re-layouts  7.83 us

profile of v3, /device:TPU:0, one launch (start us, length us, event | category | flops | bytes accessed | tf_op | source)
XLA Modules:
  0.0 46.2 jit_solution(126058461822951112)
XLA Ops:
  0.0 0.0 copy-start
  0.0 1.6 %copy-done = bf16[1,4096,256]{2,1,0:T(8,128)(2,1)S(1)} copy-done((bf16[1,4096,256]{2,1,0:T(8,128)(2,1)S(1)}, bf16[1,4096,256]{2,1,0:T(8,128)(2,1)}, u32[]{:S(2)}) %copy-start) | copy-done | bytes 2097176
  1.6 0.0 copy-start.1
  1.6 1.6 %copy-done.1 = bf16[1,4096,256]{2,1,0:T(8,128)(2,1)S(1)} copy-done((bf16[1,4096,256]{2,1,0:T(8,128)(2,1)S(1)}, bf16[1,4096,256]{2,1,0:T(8,128)(2,1)}, u32[]{:S(2)}) %copy-start.1) | copy-done | bytes 2097176
  3.2 0.0 copy-start.2
  3.2 1.6 %copy-done.2 = bf16[1,256,4096]{2,1,0:T(8,128)(2,1)S(1)} copy-done((bf16[1,256,4096]{2,1,0:T(8,128)(2,1)S(1)}, bf16[1,256,4096]{2,1,0:T(8,128)(2,1)}, u32[]{:S(2)}) %copy-start.2) | copy-done | bytes 2097176
  4.8 0.0 copy-start.3
  4.8 1.0 %copy-done.3 = bf16[64,4096]{1,0:T(8,128)(2,1)S(1)} copy-done((bf16[64,4096]{1,0:T(8,128)(2,1)S(1)}, bf16[64,4096]{1,0:T(8,128)(2,1)}, u32[]{:S(2)}) %copy-start.3) | copy-done | bytes 524312
  5.8 0.0 copy-start.4
  5.8 0.7 %copy-done.4 = s32[64,2]{0,1:T(2,128)S(1)} copy-done((s32[64,2]{0,1:T(2,128)S(1)}, s32[64,2]{0,1:T(2,128)}, u32[]{:S(2)}) %copy-start.4) | copy-done | bytes 536
  6.5 0.0 copy-start.5
  6.5 0.7 %copy-done.5 = f32[64,2]{0,1:T(2,128)S(1)} copy-done((f32[64,2]{0,1:T(2,128)S(1)}, f32[64,2]{0,1:T(2,128)}, u32[]{:S(2)}) %copy-start.5) | copy-done | bytes 536
  7.2 38.3 %shard_map.64 = bf16[4,16,1024]{2,1,0:T(8,128)(2,1)S(1)} custom-call(bf16[4,16,4096]{2,1,0:T(8,128)(2,1)S(1)} %bitcast.4, s32[2,64]{1,0:T(2,128)S(1)} %bitcast.6, f32[2,64]{1,0:T(2,128)S(1)} %bitcast.7, bf16[1,4096,256]{2,1,0:T(8,128)(2,1)S(1)} %copy-done, bf16[1,4096,256]{2,1,0:T(8,128)(2,1)S(1)} %copy-done.1, bf16[1,256,4096]{2,1,0:T(8,128)(2,1)S(1)} %copy-done.2), custom_call_target="tpu_custom_call" | custom-call | flops 1610612736 | bytes 6291456 | tf_op jit(solution)/shard_map/pallas_call | solution.py:278
  45.5 0.7 %copy.8 = bf16[64,1024]{1,0:T(8,128)(2,1)} copy(bf16[64,1024]{1,0:T(8,128)(2,1)S(1)} %bitcast.5) | data formatting | bytes 262144
Async XLA Ops:
  0.0 1.6 %copy-start = (bf16[1,4096,256]{2,1,0:T(8,128)(2,1)S(1)}, bf16[1,4096,256]{2,1,0:T(8,128)(2,1)}, u32[]{:S(2)}) copy-start(bf16[1,4096,256]{2,1,0:T(8,128)(2,1)} %wg_hbm.1) | copy-start | bytes 6291460
  1.6 1.6 %copy-start.1 = (bf16[1,4096,256]{2,1,0:T(8,128)(2,1)S(1)}, bf16[1,4096,256]{2,1,0:T(8,128)(2,1)}, u32[]{:S(2)}) copy-start(bf16[1,4096,256]{2,1,0:T(8,128)(2,1)} %wu_hbm.1) | copy-start | bytes 6291460
  3.2 1.6 %copy-start.2 = (bf16[1,256,4096]{2,1,0:T(8,128)(2,1)S(1)}, bf16[1,256,4096]{2,1,0:T(8,128)(2,1)}, u32[]{:S(2)}) copy-start(bf16[1,256,4096]{2,1,0:T(8,128)(2,1)} %wd_hbm.1) | copy-start | bytes 6291460
  4.8 1.0 %copy-start.3 = (bf16[64,4096]{1,0:T(8,128)(2,1)S(1)}, bf16[64,4096]{1,0:T(8,128)(2,1)}, u32[]{:S(2)}) copy-start(bf16[64,4096]{1,0:T(8,128)(2,1)} %param.6) | copy-start | bytes 1572868
  5.8 0.7 %copy-start.4 = (s32[64,2]{0,1:T(2,128)S(1)}, s32[64,2]{0,1:T(2,128)}, u32[]{:S(2)}) copy-start(s32[64,2]{0,1:T(2,128)} %param.7) | copy-start | bytes 1540
  6.5 0.7 %copy-start.5 = (f32[64,2]{0,1:T(2,128)S(1)}, f32[64,2]{0,1:T(2,128)}, u32[]{:S(2)}) copy-start(f32[64,2]{0,1:T(2,128)} %param.8) | copy-start | bytes 1540

commit v4 on v3

--- a/solution.py
+++ b/solution.py
@@ -138,15 +138,20 @@
     every = [(r, s) for r in range(chunks) for s in range(PIECES)]
     passed = {(r, s): remote(spot(x, (2,), r, s), spot(x, (3,), r, s), sibling) for r, s in every}
     lent_home = remote(lend.at[0], borrowed.at[0], sibling)
-    lent_away = {(r, s): remote(lend.at[1, r, s], borrowed.at[1, r, s], sibling) for r, s in every}
-    y_copies = {(r, s): remote(y_out.at[r, s], y_in.at[r, s], across) for r, s in every}
+    passes = [(0, 1), (1, chunks - 2), (chunks - 1, 1)]
+    lent_away = [
+        remote(lend.at[1, pl.ds(first, count)], borrowed.at[1, pl.ds(first, count)], sibling)
+        for first, count in passes
+    ]
+    units = [(r, 0, PIECES) for r in range(chunks - 1)] + [(chunks - 1, s, 1) for s in range(PIECES)]
+    y_copies = {(r, s): remote(y_out.at[r, pl.ds(s, n)], y_in.at[r, pl.ds(s, n)], across) for r, s, n in units}
     z_base = number[0]
 
-    def z_copy(step, r, s, to_index):
+    def z_copy(step, r, s, n, to_index):
         row = z_base + ((step - 1) * PIECES + s) * chunks
         return pltpu.make_async_remote_copy(
-            src_ref=z_out.at[r, s, lax.rem(z + step, shards)],
-            dst_ref=z_in.at[step - 1, to_index, s],
+            src_ref=z_out.at[r, lax.rem(z + step, shards), pl.ds(s, n)],
+            dst_ref=z_in.at[step - 1, to_index, pl.ds(s, n)],
             send_sem=send_sem.at[row + r],
             recv_sem=recv_sem.at[row + to_index],
             device_id=rest[step - 1],
@@ -162,34 +167,41 @@
             jnp.where(at == lax.broadcasted_iota(jnp.int32, (count, gt.shape[2]), 1), line, 0.0), axis=1, keepdims=True
         )
 
-    def enter(slot, first, count):
-        each = count * rows_per
+    def enter(parts):
         steps = 4
         span = depth // steps
-        gate = jnp.zeros((2 * each, wg.shape[1]), jnp.float32)
-        upper = jnp.zeros((2 * each, wg.shape[1]), jnp.float32)
+        gate = upper = 0.0
         for step in range(steps):
-            piece = x[slot : slot + 2, first : first + count, :, step * span : (step + 1) * span]
-            piece = piece.reshape(2 * each, span)
-            gate += jnp.dot(piece, wg[step * span : (step + 1) * span, :], preferred_element_type=jnp.float32)
-            upper += jnp.dot(piece, wu[step * span : (step + 1) * span, :], preferred_element_type=jnp.float32)
+            at = slice(step * span, (step + 1) * span)
+            piece = jnp.concatenate(
+                [x[slot : slot + 2, a : a + n, :, at].reshape(2 * n * rows_per, span) for slot, a, n in parts], axis=0
+            )
+            gate += jnp.dot(piece, wg[at, :], preferred_element_type=jnp.float32)
+            upper += jnp.dot(piece, wu[at, :], preferred_element_type=jnp.float32)
         hidden = (gate / (1.0 + jnp.exp(-gate)) * upper).astype(jnp.bfloat16)
         scale = jnp.concatenate(
-            [gate_column(slot, first * rows_per, each), gate_column(slot + 1, first * rows_per, each)], axis=0
+            [gate_column(slot + i, a * rows_per, n * rows_per) for slot, a, n in parts for i in range(2)], axis=0
         )
         return hidden, scale
 
     cw = width // shards
     cs = cw // PIECES
 
-    def leave(entered, first, count, s, kept, given):
+    def leave(entered, parts):
         hidden, scale = entered
-        each = count * rows_per
-        for q in range(shards):
-            at = q * cw + s * cs
-            part = jnp.dot(hidden, wd[:, at : at + cs], preferred_element_type=jnp.float32) * scale
-            kept[first : first + count, s, q] = part[:each].reshape(count, rows_per, cs)
-            lend[given, first : first + count, s, q] = part[each:].astype(jnp.bfloat16).reshape(count, rows_per, cs)
+        for s in range(PIECES):
+            for q in range(shards):
+                at = q * cw + s * cs
+                part = jnp.dot(hidden, wd[:, at : at + cs], preferred_element_type=jnp.float32) * scale
+                base = 0
+                for slot, a, n in parts:
+                    each = n * rows_per
+                    mine, other = part[base : base + each], part[base + each : base + 2 * each]
+                    base += 2 * each
+                    lent = other.astype(jnp.bfloat16).reshape(n, rows_per, cs)
+                    kept, given = (own, 0) if slot == 0 else (cross, 1)
+                    kept[a : a + n, s, q] = mine.reshape(n, rows_per, cs)
+                    lend[given, a : a + n, s, q] = lent
 
     def arrive(k, s):
         direct[k, s].wait_recv()
@@ -200,64 +212,77 @@
         paired[k, s].wait_recv()
         begin(passed[half + k, s])
 
-    def to_across(r, s):
-        lent_away[r, s].wait_recv()
-        y_out[r, s] = (cross[r, s] + borrowed[1, r, s].astype(jnp.float32)).astype(jnp.bfloat16)
-        begin(y_copies[r, s])
-
-    def settle(r, s):
+    def to_across(r):
+        y_out[r] = (cross[r] + borrowed[1, r].astype(jnp.float32)).astype(jnp.bfloat16)
+        for s in sorted(s for chunk, s in y_copies if chunk == r):
+            begin(y_copies[r, s])
+
+    def settle(r, s, n):
         y_copies[r, s].wait_recv()
-        total = own[r, s] + borrowed[0, r, s].astype(jnp.float32) + y_in[r, s].astype(jnp.float32)
-        own[r, s] = total
-        z_out[r, s] = total.astype(jnp.bfloat16)
+        for i in range(s, s + n):
+            total = own[r, i] + borrowed[0, r, i].astype(jnp.float32) + y_in[r, i].astype(jnp.float32)
+            own[r, i] = total
+            for q in range(shards):
+                z_out[r, q, i] = total[q].astype(jnp.bfloat16)
         for step in range(1, shards):
-            begin(z_copy(step, r, s, lax.rem(r + half * lax.rem(step, 2), chunks)))
+            begin(z_copy(step, r, s, n, (r + half * (step % 2)) % chunks))
 
     pieces = range(PIECES)
     for i in (3, 4, 0, 1):
         loads[i].wait()
     for copy in beside + gate_copies:
         copy.wait_recv()
-    entered = enter(0, 0, chunks)
     for s in pieces:
         arrive(0, s)
+    for s in pieces:
+        passed[0, s].wait_recv()
+    parts = [(0, 0, chunks), (2, 0, 1)]
+    entered = enter(parts)
+    for k in range(1, half):
+        for s in pieces:
+            arrive(k, s)
     loads[2].wait()
-    for s in pieces:
-        leave(entered, 0, chunks, s, own, 0)
+    leave(entered, parts)
+    begin(lent_away[0])
     begin(lent_home)
-    waiting = [(k, s) for k in range(1, half) for s in pieces]
-    later = [(k, s) for k in range(half) for s in pieces]
-    settled = list(every)
-    for r in range(chunks):
-        if r < half:
-            for k, s in [spot_ for spot_ in waiting if spot_[0] == r]:
-                arrive(k, s)
-        else:
-            for k, s in [spot_ for spot_ in later if spot_[0] == r - half]:
-                arrive_pair(k, s)
+    for k in range(half - 1):
+        for s in pieces:
+            arrive_pair(k, s)
+    lent_away[0].wait_recv()
+    to_across(0)
+    for r in range(1, chunks - 1):
         for s in pieces:
             passed[r, s].wait_recv()
-        entered = enter(2, r, 1)
-        if r > 0:
-            for s in pieces:
-                to_across(r - 1, s)
-        for s in pieces:
-            leave(entered, r, 1, s, cross, 1)
-            begin(lent_away[r, s])
+    parts = [(2, 1, chunks - 2)]
+    entered = enter(parts)
+    for s in pieces:
+        arrive_pair(half - 1, s)
+    leave(entered, parts)
+    begin(lent_away[1])
+    for s in pieces:
+        passed[chunks - 1, s].wait_recv()
+    parts = [(2, chunks - 1, 1)]
+    lent_away[1].wait_recv()
+    for r in range(1, chunks - 1):
+        to_across(r)
+    entered = enter(parts)
     lent_home.wait_recv()
-    first_settled = settled.pop(0)
-    settle(*first_settled)
-    for s in pieces:
-        to_across(chunks - 1, s)
-    for r, s in settled:
-        settle(r, s)
+    settle(*units[0])
+    leave(entered, parts)
+    begin(lent_away[2])
+    lent_away[2].wait_recv()
+    to_across(chunks - 1)
+    for unit in units[1:]:
+        settle(*unit)
+    for r, s, n in units:
+        for step in range(1, shards):
+            z_copy(step, r, s, n, (r + half * (step % 2)) % chunks).wait_recv()
     for r in range(chunks):
-        for s in pieces:
-            total = own[r, s, z]
+        for i in pieces:
+            total = own[r, i, z]
             for step in range(1, shards):
-                z_copy(step, r, s, r).wait_recv()
-                total = total + z_in[step - 1, r, s].astype(jnp.float32)
-            out[lax.rem(r + half * odd, chunks), :, s * cs : (s + 1) * cs] = total.astype(jnp.bfloat16)
+                total = total + z_in[step - 1, r, i].astype(jnp.float32)
+            out[lax.rem(r + half * odd, chunks), :, i * cs : (i + 1) * cs] = total.astype(jnp.bfloat16)
     for copy in sent:
         copy.wait_send()
 
@@ -292,14 +317,14 @@
             pltpu.VMEM((2,) + block, bf16),
             pltpu.VMEM(block, bf16),
             pltpu.VMEM(block, bf16),
-            pltpu.VMEM(block, bf16),
+            pltpu.VMEM((chunks, shards, PIECES, CHUNK, cw // PIECES), bf16),
             pltpu.VMEM((shards - 1, chunks, PIECES, CHUNK, cw // PIECES), bf16),
             pltpu.SemaphoreType.DMA((5,)),
             pltpu.SemaphoreType.DMA((copies,)),
             pltpu.SemaphoreType.DMA((copies,)),
         ],
         compiler_params=pltpu.CompilerParams(
-            collective_id=0, has_side_effects=True, vmem_limit_bytes=40 * 1024 * 1024
+            collective_id=0, has_side_effects=True, vmem_limit_bytes=60 * 1024 * 1024
         ),
         cost_estimate=pl.CostEstimate(
             flops=6 * total_rows * depth * tile, bytes_accessed=6 * depth * tile, transcendentals=total_rows * tile
@@ -313,7 +338,7 @@
     tok_count = tokens.shape[0] // (groups * sides)
     per_group = shards // TPE
     capacity = 2 * tok_count * routes.shape[1] // (groups * per_group)
-    return groups == 4 and per_group == 1 and capacity >= tok_count and tok_count % (2 * CHUNK) == 0 and tokens.shape[1] % (shards * PIECES * 128) == 0
+    return groups == 4 and per_group == 1 and capacity >= tok_count and tok_count % (4 * CHUNK) == 0 and tokens.shape[1] % (shards * PIECES * 128) == 0
 
 
 def solution(mesh):

time: 46.5 us -> 41.8 us (0.90)
  local copies, waits for them, and re-layouts: 7.83 us -> 1.57 us
  Pallas kernels: 38.3 us -> 40 us
    unnamed x13 -> x1, local copies, waits for them, and re-layouts: 7.83 us -> 1.57 us
    pallas_call x1, Pallas kernels: 38.3 us -> 40 us  [dense_on_device(): pl.pallas_call(functools.partial(dense_kernel, groups, shards), out_shape...]
where the time goes in v4:
time: 41.8 us; the launch traced here: 41.6 us
  Pallas kernels  40 us (96%)
  local copies, waits for them, and re-layouts  1.57 us (4%)
    pallas_call x1, Pallas kernels, dense_on_device(): pl.pallas_call(functools.partial(dense_kernel, groups, shards), out_shape...  40 us
    unnamed x1, local copies, waits for them, and re-layouts  1.57 us

profile of v4, /device:TPU:0, one launch (start us, length us, event | category | flops | bytes accessed | tf_op | source)
XLA Modules:
  0.0 41.6 jit_solution(2097387438169757302)
XLA Ops:
  0.0 40.0 %shard_map.64 = bf16[4,16,1024]{2,1,0:T(8,128)(2,1)} custom-call(bf16[4,16,4096]{2,1,0:T(8,128)(2,1)} %bitcast.4, s32[2,64]{1,0:T(2,128)} %bitcast.6, f32[2,64]{1,0:T(2,128)} %bitcast.7, bf16[1,4096,256]{2,1,0:T(8,128)(2,1)} %wg_hbm.1, bf16[1,4096,256]{2,1,0:T(8,128)(2,1)} %wu_hbm.1, bf16[1,256,4096]{2,1,0:T(8,128)(2,1)} %wd_hbm.1), custom_call_target="tpu_custom_call" | custom-call | flops 1610612736 | bytes 6291456 | tf_op jit(solution)/shard_map/pallas_call | solution.py:303
  40.0 1.6 %copy.8 = bf16[64,1024]{1,0:T(8,128)(2,1)} copy(bf16[64,1024]{1,0:T(8,128)(2,1)} %bitcast.5) | data formatting | bytes 262144
